TPU v7x, 256 devices: a whole 4x4x8 slice. The times are simulated.
256 devices in a mesh: sta: 32 (over z_lo, x, core), tm: 8 (over z_hi, y).
Axes of the slice: x: 4, y: 4, z: 8 (z_hi: 2, z_lo: 4; z = z_hi * 4 + z_lo), core: 2. Of those that a mesh axis runs over, the one named last changes fastest.
Arguments:
- records: bfloat16 [64, 3, 4096], P('sta', None, 'tm'), may hold values from -6 to 6
- templates: bfloat16 [512, 64, 3, 150], P(None, 'sta'), may hold values from -6 to 6
- moveout: int32 [512, 64], P(None, 'sta'), may hold values from 0 to 256
- gap_start: int32 [64, 3], P('sta'), may hold values from 0 to 4095
- gap_length: int32 [64, 3], P('sta'), may hold values from 0 to 599
Outputs:
- detection: float32 [512, 4096], P('sta', 'tm')
Inputs may be any that keep to these rules, and one draw needn't show every extreme that they name: `gap_length`: each channel has one gap, counted in samples of the whole window; it may run past the window's end.
All inputs are finite; a program needn't handle non-finite values.
Results may differ from a plain program's by a relative error of at most 0.0041.
Values may be sent and summed in bfloat16 or wider, within the bound.
A program may use at most 64 MiB of HBM per device.

v0:
```python
import math

import jax
import jax.numpy as jnp
from jax import lax
from jax.sharding import PartitionSpec as P

CHANNELS = 3
TEMPLATE_LEN = 150
TEMPLATES = 512
MAXMO = 256


def passed_along(value, axis, by):
    devices = lax.axis_size(axis)
    pairs = [(i, i + by) for i in range(devices) if 0 <= i + by < devices]
    return lax.ppermute(value, axis, pairs)


def in_blocks(value, dim, devices):
    before, after = (value.shape[:dim], value.shape[dim + 1 :])
    return jnp.moveaxis(value.reshape(*before, devices, -1, *after), dim, 0)


def sum_at_owner(value, axis, dim):
    devices = lax.axis_size(axis)
    tiles = lax.all_to_all(in_blocks(value, dim, devices), axis, 0, 0, tiled=True)
    return jnp.sum(tiles, axis=0)


def hankel(extended, full_width):
    return jnp.stack(
        [extended[..., offset : offset + full_width] for offset in range(TEMPLATE_LEN)], axis=-2
    )


def whiten(extended, full_width):
    widened = hankel(extended, full_width).astype(jnp.float32)
    energy = jnp.sum(widened * widened, axis=-2, keepdims=True)
    return (widened / jnp.sqrt(jnp.maximum(energy, 1.0))).astype(jnp.bfloat16)


def unit_templates(templates):
    widened = templates.astype(jnp.float32)
    return (widened / jnp.sqrt(jnp.sum(widened * widened, axis=-1, keepdims=True) + 1e-06)).astype(
        jnp.bfloat16
    )


def gap_mask(positions, gap_start, gap_length):
    first = gap_start[..., None]
    return (positions < first) | (positions >= first + gap_length[..., None])


def shift_rows(correlation, lag_column, slice_len):
    current = correlation
    bound = MAXMO
    for level in reversed(range(MAXMO.bit_length())):
        step_size = 1 << level
        new_width = slice_len + min(step_size - 1, bound)
        moved = current[:, step_size:]
        if moved.shape[1] < new_width:
            moved = jnp.pad(moved, ((0, 0), (0, new_width - moved.shape[1])))
        else:
            pass
        kept = current[:, :new_width]
        flagged = (lag_column // step_size % 2 == 1)[:, None]
        current = jnp.where(flagged, moved, kept)
        bound = min(step_size - 1, bound)
    return current


def shards(records, templates, moveout, gap_start, gap_length):
    sta_dev = records.shape[0]
    slice_len = records.shape[2]
    halo_width = MAXMO + TEMPLATE_LEN - 1
    following = passed_along(records[:, :, :halo_width], "tm", -1)
    extended = jnp.concatenate([records, following], axis=2)
    positions = lax.axis_index("tm") * slice_len + jnp.arange(
        slice_len + halo_width, dtype=jnp.int32
    )
    kept_mask = gap_mask(positions, gap_start, gap_length)
    extended = jnp.where(kept_mask, extended, jnp.zeros_like(extended))
    full_width = slice_len + MAXMO
    lagged = whiten(extended, full_width).reshape(sta_dev, CHANNELS * TEMPLATE_LEN, full_width)
    normed = unit_templates(templates).reshape(TEMPLATES, sta_dev, CHANNELS * TEMPLATE_LEN)
    own_rows = TEMPLATES // lax.axis_size("sta")

    def add_station(station, running):
        weight_rows = lax.dynamic_index_in_dim(normed, station, 1, keepdims=False)
        station_data = lax.dynamic_index_in_dim(lagged, station, 0, keepdims=False)
        correlation = jnp.dot(weight_rows, station_data, preferred_element_type=jnp.float32)
        lag_column = lax.dynamic_index_in_dim(moveout, station, 1, keepdims=False)
        return running + shift_rows(correlation, lag_column, slice_len)

    stacked = sum_at_owner(
        lax.fori_loop(
            0,
            sta_dev,
            add_station,
            jnp.zeros((own_rows * lax.axis_size("sta"), slice_len), jnp.float32),
        ),
        "sta",
        0,
    )
    stations_all = sta_dev * lax.axis_size("sta")
    return stacked * math.sqrt(TEMPLATE_LEN / (3.0 * stations_all))


def solution(mesh):
    placed = (
        P("sta", None, "tm"),
        P(None, "sta", None, None),
        P(None, "sta"),
        P("sta", None),
        P("sta", None),
    )
    return jax.shard_map(
        shards, mesh=mesh, in_specs=placed, out_specs=P("sta", "tm"), check_vma=False
    )
```

profile of v0, /device:TPU:24, one launch (start us, length us, event | category | flops | bytes accessed | tf_op | source)
XLA Modules:
  0.0 77.4 jit_solution(2745008729430847391)
XLA Ops:
  0.0 2.8 %collective-permute-start = (bf16[2,3,405]{2,0,1:T(2,128)(2,1)}, bf16[2,3,405]{2,0,1:T(2,128)(2,1)S(1)}, u32[]{:S(2)}, u32[]{:S(2)}) collective-permute-start(bf16[2,3,405]{2,0,1:T(2,128)(2,1)} %bitcast.615), channel_id=1, source_target_pairs={{1,0},{2,1},{3,2},{4,3},{5,4},{6,5},{7,6},{9,8},{10,9},{11,10},{12... | collective-permute-start | bytes 14588 | tf_op jit(solution)/shard_map/ppermute | solution.py:17
  2.8 2.1 %fusion.17 = f32[512,2,3]{0,1,2:T(2,128)S(1)} fusion(bf16[512,2,3,150]{0,1,3,2:T(2,128)(2,1)} %param.8), kind=kLoop, calls=%fused_computation.92 | loop fusion | flops 1379328 | bytes 933888 | tf_op jit(solution)/shard_map/reduce_sum | solution.py:45
  5.0 0.7 fusion.18
  6.1 5.8 %collective-permute-done = bf16[2,3,405]{2,0,1:T(2,128)(2,1)S(1)} collective-permute-done((bf16[2,3,405]{2,0,1:T(2,128)(2,1)}, bf16[2,3,405]{2,0,1:T(2,128)(2,1)S(1)}, u32[]{:S(2)}, u32[]{:S(2)}) %collective-permute-start) | collective-permute-done | bytes 4892 | tf_op jit(solution)/shard_map/ppermute | solution.py:17
  25.4 1.5 %fusion.15 = f32[2,3,768]{2,0,1:T(2,128)S(1)} fusion(bf16[2,3,150,768]{3,0,1,2:T(2,128)(2,1)S(1)} %constant_dynamic-update-slice_fusion), kind=kLoop, calls=%fused_computation.88 | loop fusion | flops 2068992 | bytes 1400832 | tf_op jit(solution)/shard_map/reduce_sum | solution.py:39
  26.9 1.1 %fusion.16 = bf16[2,3,150,768]{3,0,1,2:T(2,128)(2,1)S(1)} fusion(bf16[2,3,150,768]{3,0,1,2:T(2,128)(2,1)S(1)} %constant_dynamic-update-slice_fusion, f32[2,3,768]{2,0,1:T(2,128)S(1)} %maximum_sqrt_fusion), kind=kLoop, calls=%fused_computation.89 | loop fusion | flops 2073600 | bytes 2783232 | tf_op jit(solution)/shard_map/convert_element_type | solution.py:40
  28.2 1.5 %convert_element_type.30 = bf16[2,450,768]{2,1,0:T(8,128)(2,1)} reshape(bf16[2,3,150,768]{3,2,1,0:T(8,128)(2,1)S(1)} %copy.13) | data formatting | bytes 2764800 | tf_op jit(solution)/shard_map/convert_element_type | solution.py:40
  29.7 12.2 %while.17 = (s32[]{:T(128)}, f32[512,512]{1,0:T(8,128)S(1)}, s32[512,2]{0,1:T(2,128)S(1)}, bf16[512,2,450]{0,2,1:T(8,128)(2,1)S(1)}, bf16[2,450,768]{2,1,0:T(8,128)(2,1)}, /*index=5*/s32[]{:T(128)}, s32[]{:T(128)}) while((s32[]{:T(128)}, f32[512,512]{1,0:T(8,128)S(1)}, s32[512,2]{0,1:T(2,128)S(1)}, ...), condition=%wide.region_3.4_spmd.clone, body=%wide.region_2.3_spmd.clone.sunk | while | flops 357130240 | bytes 36771928 | solution.py:97
  29.9 1.7 %fusion.25 = f32[512,768]{1,0:T(8,128)S(1)} fusion(bf16[2,450,768]{2,1,0:T(8,128)(2,1)} %get-tuple-element.290, s32[]{:T(128)} %get-tuple-element.279, bf16[512,2,450]{0,2,1:T(8,128)(2,1)S(1)} %get-tuple-element.289), kind=kOutput, calls=%fused_computation.10.clone.1 | convolution fusion | flops 353894400 | bytes 2741248 | tf_op jit(solution)/shard_map/while/body/eval_jaxpr/dot_general | solution.py:92
  32.1 0.5 slice_select_fusion.19
  32.6 0.5 slice_select_fusion.20
  33.1 0.5 slice_select_fusion.21
  33.6 0.5 slice_select_fusion.22
  34.1 0.5 slice_select_fusion.23
  34.6 0.5 slice_select_fusion.24
  35.1 0.7 fusion.26
  36.0 1.7 %fusion.25 = f32[512,768]{1,0:T(8,128)S(1)} fusion(bf16[2,450,768]{2,1,0:T(8,128)(2,1)} %get-tuple-element.290, s32[]{:T(128)} %get-tuple-element.279, bf16[512,2,450]{0,2,1:T(8,128)(2,1)S(1)} %get-tuple-element.289), kind=kOutput, calls=%fused_computation.10.clone.1 | convolution fusion | flops 353894400 | bytes 2741248 | tf_op jit(solution)/shard_map/while/body/eval_jaxpr/dot_general | solution.py:92
  38.2 0.5 slice_select_fusion.19
  38.7 0.5 slice_select_fusion.20
  39.2 0.5 slice_select_fusion.21
  39.7 0.5 slice_select_fusion.22
  41.3 0.7 fusion.26
  41.9 34.8 %all_to_all.5 = f32[32,16,512]{2,1,0:T(8,128)S(1)} all-to-all(f32[32,16,512]{2,1,0:T(8,128)S(1)} %bitcast.613), channel_id=1, replica_groups=mesh['sta'=32,'tm'=8] {'sta'}, dimensions={0} | all-to-all | bytes 2097152 | tf_op jit(solution)/shard_map/all_to_all | solution.py:27
  76.8 0.6 broadcast_multiply_fusion
  (181 shorter events, 16.1 us)
Async XLA Ops:
  0.0 5.0 %copy-start = (bf16[512,2,3,150]{0,1,3,2:T(2,128)(2,1)S(1)}, bf16[512,2,3,150]{0,1,3,2:T(2,128)(2,1)}, u32[]{:S(2)}) copy-start(bf16[512,2,3,150]{0,1,3,2:T(2,128)(2,1)} %param.8) | copy-start | bytes 2764804
  0.0 11.9 %collective-permute-start = (bf16[2,3,405]{2,0,1:T(2,128)(2,1)}, bf16[2,3,405]{2,0,1:T(2,128)(2,1)S(1)}, u32[]{:S(2)}, u32[]{:S(2)}) collective-permute-start(bf16[2,3,405]{2,0,1:T(2,128)(2,1)} %bitcast.615), channel_id=1, source_target_pairs={{1,0},{2,1},{3,2},{4,3},{5,4},{6,5},{7,6},{9,8},{10,9},{11,10},{12... | collective-permute-start | bytes 14588 | tf_op jit(solution)/shard_map/ppermute | solution.py:17
  2.8 3.0 %copy-start.3 = (s32[2,3]{1,0:T(2,128)S(1)}, s32[2,3]{1,0:T(2,128)}, u32[]{:S(2)}) copy-start(s32[2,3]{1,0:T(2,128)} %param.10) | copy-start | bytes 76
  2.8 3.1 %copy-start.4 = (s32[2,3]{1,0:T(2,128)S(1)}, s32[2,3]{1,0:T(2,128)}, u32[]{:S(2)}) copy-start(s32[2,3]{1,0:T(2,128)} %param.11) | copy-start | bytes 76
  5.7 6.2 %copy-start.2 = (bf16[2,3,512]{2,0,1:T(2,128)(2,1)S(1)}, bf16[2,3,512]{2,0,1:T(2,128)(2,1)}, u32[]{:S(2)}) copy-start(bf16[2,3,512]{2,0,1:T(2,128)(2,1)} %param.7) | copy-start | bytes 18436
  28.2 1.5 %copy-start.1 = (s32[512,2]{0,1:T(2,128)S(1)}, s32[512,2]{0,1:T(2,128)}, u32[]{:S(2)}) copy-start(s32[512,2]{0,1:T(2,128)} %param.9) | copy-start | bytes 12292
where the time goes:
time: 78.5 us; the launch traced here: 77.4 us
  blocking collectives  34.8 us (44%)
  local copies, waits for them, and re-layouts  15.3 us (19%)
  other arithmetic  14.6 us (19%)
  waiting for transfers between devices  5.76 us (7%)
  matrix products  3.41 us (4%)
  starting transfers between devices  2.77 us (4%)
    all_to_all x1, blocking collectives, sum_at_owner(): lax.all_to_all(in_blocks(value, dim, devices), axis, 0, 0, tiled=True)  34.8 us
    unnamed x160, local copies, waits for them, and re-layouts  13.1 us
    select_n x16, other arithmetic, shift_rows(): current = jnp.where(flagged, moved, kept)  6.7 us
    ppermute x1, waiting for transfers between devices, passed_along(): return lax.ppermute(value, axis, pairs)  5.76 us
    dot_general x2, matrix products, add_station(): jnp.dot(weight_rows, station_data, preferred_element_type=jnp.float32)  3.41 us
    ppermute x1, starting transfers between devices, passed_along(): return lax.ppermute(value, axis, pairs)  2.77 us
    reduce_sum x1, other arithmetic, unit_templates(): jnp.sum(widened * widened, axis=-1, keepdims=True) + 1e-06  2.15 us
    convert_element_type x2, local copies, waits for them, and re-layouts, whiten(): return (widened / jnp.sqrt(jnp.maximum(energy, 1.0))).astype(jnp.bfloat16)  1.65 us
  transfers between devices with their start and end apart: 1, of which 1 were waited for; matrix products, arithmetic and copies ran while one was open for 4% of the time, Pallas kernels for 0%

commit v1 on v0

v1 whole, which is shorter than its diff:
```python
import functools
import math

import jax
import jax.numpy as jnp
from jax import lax
from jax.experimental import pallas as pl
from jax.experimental.pallas import tpu as pltpu
from jax.sharding import PartitionSpec as P

CHANNELS = 3
TEMPLATE_LEN = 150
TEMPLATES = 512
MAXMO = 256
NT = 4096
SLICE = 512
WIDE = 1024
FULL = SLICE + MAXMO
ROWS = 160
DEPTH = 512
MESH = pl.DeviceIdType.MESH


def kernel(
    scale,
    templates,
    records,
    moveout,
    gap_start,
    gap_length,
    out,
    packed,
    unit32,
    unit_t,
    own,
    halo,
    moves,
    series,
    rolled,
    inverse,
    hankel,
    corr,
    lag,
    half_send,
    half_recv,
    half_own,
    x_send,
    x_recv,
    x_own,
    z_send,
    z_recv,
    local_sem,
    halo_sem,
    half_sem,
    x_sem,
    z_sem,
):
    sta = lax.axis_index("sta")
    tm = lax.axis_index("tm")
    core = lax.rem(sta, 2)
    xx = lax.rem(sta // 2, 4)
    zz = sta // 8

    def at(z, x, c):
        return z * 8 + x * 2 + c

    sibling = at(zz, xx, 1 - core)
    x_peers = [at(zz, lax.rem(xx + d, 4), core) for d in range(1, 4)]
    z_peers = [at(lax.rem(zz + d, 4), xx, core) for d in range(1, 4)]

    barrier = pltpu.get_barrier_semaphore()
    pl.semaphore_signal(
        barrier, inc=1, device_id={"tm": lax.rem(tm + 1, 8)}, device_id_type=MESH
    )
    for peer in [sibling] + x_peers + z_peers:
        pl.semaphore_signal(barrier, inc=1, device_id={"sta": peer}, device_id_type=MESH)

    loads = [
        pltpu.make_async_copy(records, own, local_sem.at[0]),
        pltpu.make_async_copy(moveout, moves, local_sem.at[1]),
        pltpu.make_async_copy(templates, packed, local_sem.at[2]),
    ]
    for load in loads:
        load.start()

    pl.semaphore_wait(barrier, 8)
    halo_copy = pltpu.make_async_remote_copy(
        src_ref=records,
        dst_ref=halo,
        send_sem=halo_sem.at[0],
        recv_sem=halo_sem.at[1],
        device_id={"tm": lax.rem(tm + 7, 8)},
        device_id_type=MESH,
    )
    halo_copy.start()

    for load in loads:
        load.wait()

    for s in range(2):
        for q in range(4):
            line = moves[s : s + 1, 128 * q : 128 * (q + 1)]
            lag[s, 128 * q : 128 * (q + 1), :] = jnp.broadcast_to(line, (128, 128)).T

    unit32[3600:3680, :] = jnp.zeros((80, 128), jnp.float32)
    for c in range(CHANNELS):
        wide = packed[1200 * c : 1200 * (c + 1), :].astype(jnp.float32).reshape(150, 8, 128)
        norm = 1.0 / jnp.sqrt(jnp.sum(wide * wide, axis=0, keepdims=True) + 1e-06)
        unit32[1200 * c : 1200 * (c + 1), :] = (wide * norm).reshape(1200, 128)
    row = lax.broadcasted_iota(jnp.int32, (ROWS, 128), 0)
    for s in range(2):
        for q in range(4):
            parts = []
            for c in range(CHANNELS):
                taken = unit32[pl.ds(1200 * c + 2 * q + s, ROWS, stride=8), :]
                parts.append(jnp.where(row < TEMPLATE_LEN, taken, 0.0))
            parts.append(jnp.zeros((DEPTH - 3 * ROWS, 128), jnp.float32))
            block = jnp.concatenate(parts, axis=0).astype(jnp.bfloat16)
            unit_t[s, 128 * q : 128 * (q + 1), :] = block.T

    halo_copy.wait()

    series[...] = jnp.zeros_like(series)
    for c in range(CHANNELS):
        series[2 * c : 2 * c + 2, 0:SLICE] = own[c].astype(jnp.float32)
        series[2 * c : 2 * c + 2, SLICE:WIDE] = halo[c].astype(jnp.float32)
    line = lax.broadcasted_iota(jnp.int32, (8, WIDE), 0)
    position = lax.broadcasted_iota(jnp.int32, (8, WIDE), 1) + tm * SLICE
    first = jnp.zeros((8, WIDE), jnp.int32)
    length = jnp.zeros((8, WIDE), jnp.int32)
    for s in range(2):
        for c in range(CHANNELS):
            first = jnp.where(line == 2 * c + s, gap_start[s, c], first)
            length = jnp.where(line == 2 * c + s, gap_length[s, c], length)
    kept = ((position < first) | (position >= first + length)) & (position < NT)
    masked = jnp.where(kept, series[...], 0.0)

    def ahead(value, by):
        return pltpu.roll(value, WIDE - by, 1)

    for r in range(8):
        moved = masked if r == 0 else ahead(masked, r)
        for b in range(8):
            rolled[b, 8 * r : 8 * (r + 1), :] = moved[:, 128 * b : 128 * (b + 1)]
    sums = {1: masked * masked}
    for power in range(7):
        width = 1 << power
        sums[2 * width] = sums[width] + ahead(sums[width], width)
    energy = (sums[128] + ahead(sums[16], 128)) + (ahead(sums[4], 144) + ahead(sums[2], 148))
    inverse[...] = (1.0 / jnp.sqrt(jnp.maximum(energy, 1.0)))[:, :FULL]

    for s in range(2):
        hankel[s, 3 * ROWS : DEPTH, :] = jnp.zeros((DEPTH - 3 * ROWS, FULL), jnp.bfloat16)
        for c in range(CHANNELS):
            eight = jnp.concatenate(
                [rolled[b, pl.ds(2 * c + s, 8, stride=8), :] for b in range(8)], axis=1
            )
            weight = inverse[2 * c + s : 2 * c + s + 1, :]
            for a in range(ROWS // 16):
                top = eight if a == 0 else ahead(eight, 16 * a)
                low = ahead(eight, 16 * a + 8)
                both = jnp.concatenate([top[:, :FULL] * weight, low[:, :FULL] * weight], axis=0)
                hankel[s, ROWS * c + 16 * a : ROWS * c + 16 * (a + 1), :] = both.astype(
                    jnp.bfloat16
                )

    lane = lax.broadcasted_iota(jnp.int32, (16, 128), 1)

    def correlate(side, store):
        for s in range(2):
            rows = [
                unit_t[s, pl.ds(pl.multiple_of(32 * g + 16 * side, 16), 16), :] for g in range(16)
            ]
            corr[s] = jnp.dot(
                jnp.concatenate(rows, axis=0), hankel[s], preferred_element_type=jnp.float32
            )

        def group(g, carry):
            base = pl.multiple_of(16 * g, 16)
            start = pl.multiple_of(32 * g + 16 * side, 16)
            total = [None] * 4
            for s in range(2):
                move = lag[s, pl.ds(start, 16), :]
                near = move <= lane
                middle = move <= lane + 128
                index = (lane + move) & 127
                pieces = [corr[s, pl.ds(base, 16), 128 * j : 128 * (j + 1)] for j in range(6)]
                for j in range(4):
                    mixed = jnp.where(
                        near, pieces[j], jnp.where(middle, pieces[j + 1], pieces[j + 2])
                    )
                    moved = jnp.take_along_axis(mixed, index, axis=1, mode="promise_in_bounds")
                    total[j] = moved if s == 0 else total[j] + moved
            store(g, jnp.concatenate(total, axis=1))
            return carry

        lax.fori_loop(0, 16, group, 0)

    def to_send(g, value):
        half_send[g // 4, lax.rem(g, 4)] = value.astype(jnp.bfloat16)

    def to_own(g, value):
        half_own[g // 4, lax.rem(g, 4)] = value

    correlate(1 - core, to_send)
    half_copy = pltpu.make_async_remote_copy(
        src_ref=half_send,
        dst_ref=half_recv,
        send_sem=half_sem.at[0],
        recv_sem=half_sem.at[1],
        device_id={"sta": sibling},
        device_id_type=MESH,
    )
    half_copy.start()
    correlate(core, to_own)
    half_copy.wait()

    x_copies = []
    for d in (2, 1, 3):
        target = lax.rem(xx + d, 4)
        x_send[d - 1] = (
            half_own[:, target] + half_recv[:, target].astype(jnp.float32)
        ).astype(jnp.bfloat16)
        copy = pltpu.make_async_remote_copy(
            src_ref=x_send.at[d - 1],
            dst_ref=x_recv.at[d - 1],
            send_sem=x_sem.at[0, d - 1],
            recv_sem=x_sem.at[1, d - 1],
            device_id={"sta": x_peers[d - 1]},
            device_id_type=MESH,
        )
        copy.start()
        x_copies.append(copy)
    x_own[...] = half_own[:, xx] + half_recv[:, xx].astype(jnp.float32)
    for copy in x_copies:
        copy.wait()

    def over_x(z):
        total = x_own[z]
        for d in range(3):
            total = total + x_recv[d, z].astype(jnp.float32)
        return total

    z_copies = []
    for d in (2, 1, 3):
        z_send[d - 1] = over_x(lax.rem(zz + d, 4)).astype(jnp.bfloat16)
        copy = pltpu.make_async_remote_copy(
            src_ref=z_send.at[d - 1],
            dst_ref=z_recv.at[d - 1],
            send_sem=z_sem.at[0, d - 1],
            recv_sem=z_sem.at[1, d - 1],
            device_id={"sta": z_peers[d - 1]},
            device_id_type=MESH,
        )
        copy.start()
        z_copies.append(copy)
    total = over_x(zz)
    for copy in z_copies:
        copy.wait()
    for d in range(3):
        total = total + z_recv[d].astype(jnp.float32)
    out[...] = total * scale


def shards(records, templates, moveout, gap_start, gap_length):
    stations = records.shape[0] * lax.axis_size("sta")
    scale = math.sqrt(TEMPLATE_LEN / (3.0 * stations))
    lines = jnp.transpose(templates, (2, 3, 1, 0)).reshape(450, 2, 4, 128)
    lines = jnp.transpose(lines, (0, 2, 1, 3)).reshape(3600, 128)
    whole = pl.BlockSpec(memory_space=pl.ANY)
    scalars = pl.BlockSpec(memory_space=pltpu.SMEM)
    return pl.pallas_call(
        functools.partial(kernel, scale),
        out_shape=jax.ShapeDtypeStruct((16, SLICE), jnp.float32),
        in_specs=[whole, whole, whole, scalars, scalars],
        out_specs=pl.BlockSpec(memory_space=pltpu.VMEM),
        scratch_shapes=[
            pltpu.VMEM((3600, 128), jnp.bfloat16),
            pltpu.VMEM((3680, 128), jnp.float32),
            pltpu.VMEM((2, TEMPLATES, DEPTH), jnp.bfloat16),
            pltpu.VMEM((3, 2, SLICE), jnp.bfloat16),
            pltpu.VMEM((3, 2, SLICE), jnp.bfloat16),
            pltpu.VMEM((2, TEMPLATES), jnp.int32),
            pltpu.VMEM((8, WIDE), jnp.float32),
            pltpu.VMEM((8, 64, 128), jnp.float32),
            pltpu.VMEM((8, FULL), jnp.float32),
            pltpu.VMEM((2, DEPTH, FULL), jnp.bfloat16),
            pltpu.VMEM((2, 256, FULL), jnp.float32),
            pltpu.VMEM((2, TEMPLATES, 128), jnp.int32),
            pltpu.VMEM((4, 4, 16, SLICE), jnp.bfloat16),
            pltpu.VMEM((4, 4, 16, SLICE), jnp.bfloat16),
            pltpu.VMEM((4, 4, 16, SLICE), jnp.float32),
            pltpu.VMEM((3, 4, 16, SLICE), jnp.bfloat16),
            pltpu.VMEM((3, 4, 16, SLICE), jnp.bfloat16),
            pltpu.VMEM((4, 16, SLICE), jnp.float32),
            pltpu.VMEM((3, 16, SLICE), jnp.bfloat16),
            pltpu.VMEM((3, 16, SLICE), jnp.bfloat16),
            pltpu.SemaphoreType.DMA((3,)),
            pltpu.SemaphoreType.DMA((2,)),
            pltpu.SemaphoreType.DMA((2,)),
            pltpu.SemaphoreType.DMA((2, 3)),
            pltpu.SemaphoreType.DMA((2, 3)),
        ],
        compiler_params=pltpu.CompilerParams(
            collective_id=0, has_side_effects=True, vmem_limit_bytes=40 * 1024 * 1024
        ),
    )(lines, jnp.transpose(records, (1, 0, 2)), jnp.transpose(moveout, (1, 0)), gap_start, gap_length)


def solution(mesh):
    placed = (
        P("sta", None, "tm"),
        P(None, "sta", None, None),
        P(None, "sta"),
        P("sta", None),
        P("sta", None),
    )
    return jax.shard_map(
        shards, mesh=mesh, in_specs=placed, out_specs=P("sta", "tm"), check_vma=False
    )
```

time: 78.5 us -> 32 us (0.41); the launches traced: 77.4 us -> 31.8 us
  blocking collectives: 34.8 us -> 0 us
  Pallas kernels: 0 us -> 27.9 us
  other arithmetic: 14.6 us -> 0 us
  local copies, waits for them, and re-layouts: 15.3 us -> 3.86 us
  waiting for transfers between devices: 5.76 us -> 0 us
  matrix products: 3.41 us -> 0 us
  starting transfers between devices: 2.77 us -> 0 us
    all_to_all x1 -> x0, blocking collectives: 34.8 us -> none  [sum_at_owner(): lax.all_to_all(in_blocks(value, dim, devices), axis, 0, 0, tiled=True)]
    pallas_call x0 -> x1, Pallas kernels: none -> 27.9 us  [shards(): pl.pallas_call(functools.partial(kernel, scale), out_shape=jax.ShapeDtype...]
    unnamed x160 -> x11, local copies, waits for them, and re-layouts: 13.1 us -> 3.86 us
    select_n x17 -> x0, other arithmetic: 6.79 us -> none  [the longest x16 6.7 us: shift_rows(): current = jnp.where(flagged, moved, kept)]
    ppermute x1 -> x0, waiting for transfers between devices: 5.76 us -> none  [passed_along(): return lax.ppermute(value, axis, pairs)]
    reduce_sum x3 -> x0, other arithmetic: 3.71 us -> none  [the longest x1 2.15 us: unit_templates(): jnp.sum(widened * widened, axis=-1, keepdims=True) + 1e-06]
    dot_general x2 -> x0, matrix products: 3.41 us -> none  [add_station(): jnp.dot(weight_rows, station_data, preferred_element_type=jnp.float32)]
    ppermute x1 -> x0, starting transfers between devices: 2.77 us -> none  [passed_along(): return lax.ppermute(value, axis, pairs)]
  transfers between devices with their start and end apart: 1 -> 0, of which waited for: 1 -> 0; matrix products, arithmetic and copies ran while one was open for 4% -> 0% of each run, Pallas kernels for 0% -> 0%
where the time goes in v1:
time: 32 us; the launch traced here: 31.8 us
  Pallas kernels  27.9 us (87%)
  local copies, waits for them, and re-layouts  3.86 us (12%)
    pallas_call x1, Pallas kernels, shards(): pl.pallas_call(functools.partial(kernel, scale), out_shape=jax.ShapeDtype...  27.9 us
    unnamed x11, local copies, waits for them, and re-layouts  3.86 us

profile of v1, /device:TPU:24, one launch (start us, length us, event | category | flops | bytes accessed | tf_op | source)
XLA Modules:
  0.0 31.8 jit_solution(16555063490547109589)
XLA Ops:
  0.0 0.0 copy-start.2
  0.0 0.0 copy-start.3
  0.0 0.7 %copy-done.2 = s32[512,2]{0,1:T(2,128)S(1)} copy-done((s32[512,2]{0,1:T(2,128)S(1)}, s32[512,2]{0,1:T(2,128)}, u32[]{:S(2)}) %copy-start.2) | copy-done | bytes 4120
  0.7 0.0 copy-done.3
  0.7 0.0 copy-start
  0.7 1.2 %copy-done = bf16[512,2,3,150]{0,1,3,2:T(2,128)(2,1)S(1)} copy-done((bf16[512,2,3,150]{0,1,3,2:T(2,128)(2,1)S(1)}, bf16[512,2,3,150]{0,1,3,2:T(2,128)(2,1)}, u32[]{:S(2)}) %copy-start) | copy-done | bytes 921624
  1.9 0.0 copy-start.1
  1.9 0.7 %copy-done.1 = bf16[2,3,512]{2,0,1:T(2,128)(2,1)S(1)} copy-done((bf16[2,3,512]{2,0,1:T(2,128)(2,1)S(1)}, bf16[2,3,512]{2,0,1:T(2,128)(2,1)}, u32[]{:S(2)}) %copy-start.1) | copy-done | bytes 6168
  2.6 0.0 copy-start.4
  2.6 0.7 %copy-done.4 = s32[2,3]{1,0:T(2,128)S(1)} copy-done((s32[2,3]{1,0:T(2,128)S(1)}, s32[2,3]{1,0:T(2,128)}, u32[]{:S(2)}) %copy-start.4) | copy-done | bytes 48
  3.2 27.9 %shard_map.55 = f32[16,512]{1,0:T(8,128)S(1)} custom-call(bf16[3600,128]{1,0:T(8,128)(2,1)S(1)} %bitcast.9, bf16[3,2,512]{2,1,0:T(2,128)(2,1)S(1)} %bitcast.10, s32[2,512]{1,0:T(2,128)S(1)} %bitcast.11, s32[2,3]{1,0:T(2,128)S(1)} %copy-done.3, s32[2,3]{1,0:T(2,128)S(1)} %copy-done.4), custom_call_target="tpu_custom_call" | custom-call | tf_op jit(solution)/shard_map/pallas_call | solution.py:272
  31.2 0.6 %copy.8 = f32[16,512]{1,0:T(8,128)} copy(f32[16,512]{1,0:T(8,128)S(1)} %shard_map.55) | data formatting | bytes 65536
Async XLA Ops:
  0.0 0.7 %copy-start.2 = (s32[512,2]{0,1:T(2,128)S(1)}, s32[512,2]{0,1:T(2,128)}, u32[]{:S(2)}) copy-start(s32[512,2]{0,1:T(2,128)} %param.7) | copy-start | bytes 12292
  0.0 0.7 %copy-start.3 = (s32[2,3]{1,0:T(2,128)S(1)}, s32[2,3]{1,0:T(2,128)}, u32[]{:S(2)}) copy-start(s32[2,3]{1,0:T(2,128)} %gap_start.1) | copy-start | bytes 76
  0.7 1.2 %copy-start = (bf16[512,2,3,150]{0,1,3,2:T(2,128)(2,1)S(1)}, bf16[512,2,3,150]{0,1,3,2:T(2,128)(2,1)}, u32[]{:S(2)}) copy-start(bf16[512,2,3,150]{0,1,3,2:T(2,128)(2,1)} %param.6) | copy-start | bytes 2764804
  1.9 0.7 %copy-start.1 = (bf16[2,3,512]{2,0,1:T(2,128)(2,1)S(1)}, bf16[2,3,512]{2,0,1:T(2,128)(2,1)}, u32[]{:S(2)}) copy-start(bf16[2,3,512]{2,0,1:T(2,128)(2,1)} %param.5) | copy-start | bytes 18436
  2.6 0.7 %copy-start.4 = (s32[2,3]{1,0:T(2,128)S(1)}, s32[2,3]{1,0:T(2,128)}, u32[]{:S(2)}) copy-start(s32[2,3]{1,0:T(2,128)} %gap_length.1) | copy-start | bytes 76

commit v2 on v1

v2 whole, which is shorter than its diff:
```python
import functools
import math

import jax
import jax.numpy as jnp
from jax import lax
from jax.experimental import pallas as pl
from jax.experimental.pallas import tpu as pltpu
from jax.sharding import PartitionSpec as P

CHANNELS = 3
TEMPLATE_LEN = 150
TEMPLATES = 512
MAXMO = 256
NT = 4096
SLICE = 512
WIDE = 1024
FULL = SLICE + MAXMO
NEAR = 256
ROWS = 160
DEPTH = 512
MESH = pl.DeviceIdType.MESH


def paired(index, by):
    return (index, index + 1 - 2 * lax.rem(index, 2), lax.rem(index + 2, 4), 3 - index)[by]


def kernel(
    scale,
    templates,
    records,
    moveout,
    gap_start,
    gap_length,
    out,
    packed,
    unit32,
    unit_t,
    own,
    halo,
    moves,
    gaps,
    series,
    rolled,
    inverse,
    hankel,
    corr,
    lag,
    half_send,
    half_recv,
    half_own,
    part_send,
    part_recv,
    part_own,
    local_sem,
    halo_sem,
    half_sem,
    send_sem,
    recv_sem,
):
    sta = lax.axis_index("sta")
    tm = lax.axis_index("tm")
    core = lax.rem(sta, 2)
    xx = lax.rem(sta // 2, 4)
    zz = sta // 8
    zs = [paired(zz, a) for a in range(4)]
    xs = [paired(xx, b) for b in range(4)]

    def at(a, b, c):
        return {"sta": zs[a] * 8 + xs[b] * 2 + c}

    sibling = at(0, 0, 1 - core)
    barrier = pltpu.get_barrier_semaphore()

    @pl.when(tm < 7)
    def _():
        pl.semaphore_signal(
            barrier, inc=1, device_id={"tm": lax.rem(tm + 1, 8)}, device_id_type=MESH
        )

    for a in (3, 2, 1, 0):
        for b in (2, 1, 3, 0):
            if (a, b) != (0, 0):
                pl.semaphore_signal(barrier, inc=1, device_id=at(a, b, core), device_id_type=MESH)
    pl.semaphore_signal(barrier, inc=1, device_id=sibling, device_id_type=MESH)

    loads = [
        pltpu.make_async_copy(records, own, local_sem.at[0]),
        pltpu.make_async_copy(gap_start, gaps.at[0], local_sem.at[1]),
        pltpu.make_async_copy(gap_length, gaps.at[1], local_sem.at[2]),
        pltpu.make_async_copy(moveout, moves, local_sem.at[3]),
        pltpu.make_async_copy(templates, packed, local_sem.at[4]),
    ]
    for load in loads:
        load.start()

    @pl.when(tm == 7)
    def _():
        halo[...] = jnp.zeros_like(halo)

    for load in loads[:4]:
        load.wait()

    for s in range(2):
        for q in range(4):
            line = moves[s : s + 1, 128 * q : 128 * (q + 1)]
            lag[s, 128 * q : 128 * (q + 1), :] = jnp.broadcast_to(line, (128, 128)).T

    pl.semaphore_wait(barrier, 16 + jnp.where(tm > 0, 1, 0))
    halo_copy = pltpu.make_async_remote_copy(
        src_ref=own,
        dst_ref=halo,
        send_sem=halo_sem.at[0],
        recv_sem=halo_sem.at[1],
        device_id={"tm": lax.rem(tm + 7, 8)},
        device_id_type=MESH,
    )

    @pl.when(tm > 0)
    def _():
        halo_copy.start()

    loads[4].wait()

    unit32[3600:3680, :] = jnp.zeros((80, 128), jnp.float32)
    for c in range(CHANNELS):
        wide = packed[1200 * c : 1200 * (c + 1), :].astype(jnp.float32).reshape(150, 8, 128)
        norm = 1.0 / jnp.sqrt(jnp.sum(wide * wide, axis=0, keepdims=True) + 1e-06)
        unit32[1200 * c : 1200 * (c + 1), :] = (wide * norm).reshape(1200, 128)
    row = lax.broadcasted_iota(jnp.int32, (ROWS, 128), 0)
    for s in range(2):
        for q in range(4):
            parts = []
            for c in range(CHANNELS):
                taken = unit32[pl.ds(1200 * c + 2 * q + s, ROWS, stride=8), :]
                parts.append(jnp.where(row < TEMPLATE_LEN, taken, 0.0))
            parts.append(jnp.zeros((DEPTH - 3 * ROWS, 128), jnp.float32))
            block = jnp.concatenate(parts, axis=0).astype(jnp.bfloat16)
            unit_t[s, 128 * q : 128 * (q + 1), :] = block.T

    series[...] = jnp.zeros_like(series)
    for c in range(CHANNELS):
        series[2 * c : 2 * c + 2, 0:SLICE] = own[c].astype(jnp.float32)

    def spread(begin, end, base, stop):
        span = stop - base
        width = end - begin
        skip = begin - base
        line = lax.broadcasted_iota(jnp.int32, (8, span), 0)
        position = lax.broadcasted_iota(jnp.int32, (8, span), 1) + (tm * SLICE + base)
        first = jnp.zeros((8, span), jnp.int32)
        length = jnp.zeros((8, span), jnp.int32)
        for s in range(2):
            for c in range(CHANNELS):
                first = jnp.where(line == 2 * c + s, gaps[0, s, c], first)
                length = jnp.where(line == 2 * c + s, gaps[1, s, c], length)
        kept = ((position < first) | (position >= first + length)) & (position < NT)
        masked = jnp.where(kept, series[:, base:stop], 0.0)

        def ahead(value, by):
            return pltpu.roll(value, span - by, 1) if by else value

        for r in range(8):
            moved = ahead(masked, r)
            for b in range(span // 128):
                rolled[b, 8 * r : 8 * (r + 1), :] = moved[:, 128 * b : 128 * (b + 1)]
        sums = {1: masked * masked}
        for power in range(7):
            step = 1 << power
            sums[2 * step] = sums[step] + ahead(sums[step], step)
        energy = (sums[128] + ahead(sums[16], 128)) + (ahead(sums[4], 144) + ahead(sums[2], 148))
        inverse[:, begin:end] = (1.0 / jnp.sqrt(jnp.maximum(energy, 1.0)))[:, skip : skip + width]
        for s in range(2):
            hankel[s, 3 * ROWS : DEPTH, begin:end] = jnp.zeros(
                (DEPTH - 3 * ROWS, width), jnp.bfloat16
            )
            for c in range(CHANNELS):
                eight = jnp.concatenate(
                    [rolled[b, pl.ds(2 * c + s, 8, stride=8), :] for b in range(span // 128)],
                    axis=1,
                )
                weight = inverse[2 * c + s : 2 * c + s + 1, begin:end]
                for g in range(ROWS // 16):
                    pair = [
                        ahead(eight, 16 * g + 8 * h)[:, skip : skip + width] * weight
                        for h in range(2)
                    ]
                    hankel[s, ROWS * c + 16 * g : ROWS * c + 16 * (g + 1), begin:end] = (
                        jnp.concatenate(pair, axis=0).astype(jnp.bfloat16)
                    )

    def blocks(chunk):
        return [(a, b) for a in ((3, 2), (1, 0))[chunk] for b in (2, 1, 3, 0)]

    def first_row(a, b, side):
        return pl.multiple_of(128 * zs[a] + 32 * xs[b] + 16 * side, 16)

    def multiply(chunk, slot, side, begin, end):
        for s in range(2):
            rows = [unit_t[s, pl.ds(first_row(a, b, side), 16), :] for a, b in blocks(chunk)]
            corr[s, 128 * slot : 128 * (slot + 1), begin:end] = jnp.dot(
                jnp.concatenate(rows, axis=0),
                hankel[s, :, begin:end],
                preferred_element_type=jnp.float32,
            )

    lane = lax.broadcasted_iota(jnp.int32, (16, 128), 1)

    def shift(chunk, slot, side, store):
        for g, (a, b) in enumerate(blocks(chunk)):
            base = 128 * slot + 16 * g
            total = [None] * 4
            for s in range(2):
                move = lag[s, pl.ds(first_row(a, b, side), 16), :]
                near = move <= lane
                middle = move <= lane + 128
                index = (lane + move) & 127
                pieces = [corr[s, base : base + 16, 128 * j : 128 * (j + 1)] for j in range(6)]
                for j in range(4):
                    mixed = jnp.where(
                        near, pieces[j], jnp.where(middle, pieces[j + 1], pieces[j + 2])
                    )
                    moved = jnp.take_along_axis(mixed, index, axis=1, mode="promise_in_bounds")
                    total[j] = moved if s == 0 else total[j] + moved
            store(8 * chunk + g, jnp.concatenate(total, axis=1))

    def to_send(place, value):
        half_send[place] = value.astype(jnp.bfloat16)

    def to_own(place, value):
        half_own[place] = value

    def half_copy(chunk):
        return pltpu.make_async_remote_copy(
            src_ref=half_send.at[pl.ds(8 * chunk, 8)],
            dst_ref=half_recv.at[pl.ds(8 * chunk, 8)],
            send_sem=half_sem.at[0, chunk],
            recv_sem=half_sem.at[1, chunk],
            device_id=sibling,
            device_id_type=MESH,
        )

    def part_copy(a, b):
        place = 4 * a + b
        return pltpu.make_async_remote_copy(
            src_ref=part_send.at[place],
            dst_ref=part_recv.at[place],
            send_sem=send_sem.at[place],
            recv_sem=recv_sem.at[place],
            device_id=at(a, b, core),
            device_id_type=MESH,
        )

    stages = [(0, 0, 1 - core), (1, 1, 1 - core), (0, 2, core), (1, 3, core)]
    spread(0, NEAR, 0, SLICE)
    for chunk, slot, side in stages:
        multiply(chunk, slot, side, 0, NEAR)

    @pl.when(tm > 0)
    def _():
        halo_copy.wait_send()

    @pl.when(tm < 7)
    def _():
        halo_copy.wait_recv()

    for c in range(CHANNELS):
        series[2 * c : 2 * c + 2, SLICE:WIDE] = halo[c].astype(jnp.float32)
    spread(NEAR, FULL, NEAR, WIDE)

    copies = []
    for chunk, slot, side in stages:
        multiply(chunk, slot, side, NEAR, FULL)
        shift(chunk, slot, side, to_send if slot < 2 else to_own)
        copy = half_copy(chunk)
        if slot < 2:
            copy.start()
            continue
        copy.wait()
        for g, (a, b) in enumerate(blocks(chunk)):
            place = 8 * chunk + g
            value = half_own[place] + half_recv[place].astype(jnp.float32)
            if (a, b) == (0, 0):
                part_own[...] = value
            else:
                part_send[4 * a + b] = value.astype(jnp.bfloat16)
                part = part_copy(a, b)
                part.start()
                copies.append((4 * a + b, part))

    total = part_own[...]
    for place, part in copies:
        part.wait()
        total = total + part_recv[place].astype(jnp.float32)
    out[...] = total * scale


def shards(records, templates, moveout, gap_start, gap_length):
    stations = records.shape[0] * lax.axis_size("sta")
    scale = math.sqrt(TEMPLATE_LEN / (3.0 * stations))
    lines = jnp.transpose(templates, (2, 3, 1, 0)).reshape(450, 2, 4, 128)
    lines = jnp.transpose(lines, (0, 2, 1, 3)).reshape(3600, 128)
    whole = pl.BlockSpec(memory_space=pltpu.HBM)
    return pl.pallas_call(
        functools.partial(kernel, scale),
        out_shape=jax.ShapeDtypeStruct((16, SLICE), jnp.float32),
        in_specs=[whole] * 5,
        out_specs=pl.BlockSpec(memory_space=pltpu.VMEM),
        scratch_shapes=[
            pltpu.VMEM((3600, 128), jnp.bfloat16),
            pltpu.VMEM((3680, 128), jnp.float32),
            pltpu.VMEM((2, TEMPLATES, DEPTH), jnp.bfloat16),
            pltpu.VMEM((3, 2, SLICE), jnp.bfloat16),
            pltpu.VMEM((3, 2, SLICE), jnp.bfloat16),
            pltpu.VMEM((2, TEMPLATES), jnp.int32),
            pltpu.SMEM((2, 2, 3), jnp.int32),
            pltpu.VMEM((8, WIDE), jnp.float32),
            pltpu.VMEM((8, 64, 128), jnp.float32),
            pltpu.VMEM((8, FULL), jnp.float32),
            pltpu.VMEM((2, DEPTH, FULL), jnp.bfloat16),
            pltpu.VMEM((2, TEMPLATES, FULL), jnp.float32),
            pltpu.VMEM((2, TEMPLATES, 128), jnp.int32),
            pltpu.VMEM((16, 16, SLICE), jnp.bfloat16),
            pltpu.VMEM((16, 16, SLICE), jnp.bfloat16),
            pltpu.VMEM((16, 16, SLICE), jnp.float32),
            pltpu.VMEM((16, 16, SLICE), jnp.bfloat16),
            pltpu.VMEM((16, 16, SLICE), jnp.bfloat16),
            pltpu.VMEM((16, SLICE), jnp.float32),
            pltpu.SemaphoreType.DMA((5,)),
            pltpu.SemaphoreType.DMA((2,)),
            pltpu.SemaphoreType.DMA((2, 2)),
            pltpu.SemaphoreType.DMA((16,)),
            pltpu.SemaphoreType.DMA((16,)),
        ],
        compiler_params=pltpu.CompilerParams(
            collective_id=0, has_side_effects=True, vmem_limit_bytes=40 * 1024 * 1024
        ),
    )(
        *[
            pltpu.with_memory_space_constraint(value, pltpu.HBM)
            for value in (
                lines,
                jnp.transpose(records, (1, 0, 2)),
                jnp.transpose(moveout, (1, 0)),
                gap_start,
                gap_length,
            )
        ]
    )


def solution(mesh):
    placed = (
        P("sta", None, "tm"),
        P(None, "sta", None, None),
        P(None, "sta"),
        P("sta", None),
        P("sta", None),
    )
    return jax.shard_map(
        shards, mesh=mesh, in_specs=placed, out_specs=P("sta", "tm"), check_vma=False
    )
```

time: 32 us -> 25.2 us (0.79)
  Pallas kernels: 27.9 us -> 24.4 us
  local copies, waits for them, and re-layouts: 3.86 us -> 0.62 us
    pallas_call x1, Pallas kernels: 27.9 us -> 24.4 us  [shards(): pl.pallas_call(functools.partial(kernel, scale), out_shape=jax.ShapeDtype...]
    unnamed x11 -> x1, local copies, waits for them, and re-layouts: 3.86 us -> 0.62 us
where the time goes in v2:
time: 25.2 us; the launch traced here: 25.1 us
  Pallas kernels  24.4 us (97%)
  local copies, waits for them, and re-layouts  0.62 us (2%)
    pallas_call x1, Pallas kernels, shards(): pl.pallas_call(functools.partial(kernel, scale), out_shape=jax.ShapeDtype...  24.4 us
    unnamed x1, local copies, waits for them, and re-layouts  0.62 us

profile of v2, /device:TPU:24, one launch (start us, length us, event | category | flops | bytes accessed | tf_op | source)
XLA Modules:
  0.0 25.1 jit_solution(9926903117590574210)
XLA Ops:
  0.0 24.4 %shard_map.55 = f32[16,512]{1,0:T(8,128)S(1)} custom-call(bf16[3600,128]{1,0:T(8,128)(2,1)} %bitcast.9, bf16[3,2,512]{2,1,0:T(2,128)(2,1)} %bitcast.10, s32[2,512]{1,0:T(2,128)} %bitcast.11, s32[2,3]{1,0:T(2,128)} %gap_start.1, s32[2,3]{1,0:T(2,128)} %gap_length.1), custom_call_target="tpu_custom_call" | custom-call | tf_op jit(solution)/shard_map/pallas_call | solution.py:305
  24.4 0.6 %copy.8 = f32[16,512]{1,0:T(8,128)} copy(f32[16,512]{1,0:T(8,128)S(1)} %shard_map.55) | data formatting | bytes 65536

commit v3 on v2

--- a/solution.py
+++ b/solution.py
@@ -50,14 +50,16 @@
     half_send,
     half_recv,
     half_own,
-    part_send,
-    part_recv,
-    part_own,
+    x_send,
+    x_recv,
+    x_own,
+    z_send,
+    z_recv,
     local_sem,
     halo_sem,
     half_sem,
-    send_sem,
-    recv_sem,
+    x_sem,
+    z_sem,
 ):
     sta = lax.axis_index("sta")
     tm = lax.axis_index("tm")
@@ -79,10 +81,8 @@
             barrier, inc=1, device_id={"tm": lax.rem(tm + 1, 8)}, device_id_type=MESH
         )
 
-    for a in (3, 2, 1, 0):
-        for b in (2, 1, 3, 0):
-            if (a, b) != (0, 0):
-                pl.semaphore_signal(barrier, inc=1, device_id=at(a, b, core), device_id_type=MESH)
+    for a, b in ((3, 0), (2, 0), (1, 0), (0, 2), (0, 1), (0, 3)):
+        pl.semaphore_signal(barrier, inc=1, device_id=at(a, b, core), device_id_type=MESH)
     pl.semaphore_signal(barrier, inc=1, device_id=sibling, device_id_type=MESH)
 
     loads = [
@@ -107,7 +107,7 @@
             line = moves[s : s + 1, 128 * q : 128 * (q + 1)]
             lag[s, 128 * q : 128 * (q + 1), :] = jnp.broadcast_to(line, (128, 128)).T
 
-    pl.semaphore_wait(barrier, 16 + jnp.where(tm > 0, 1, 0))
+    pl.semaphore_wait(barrier, 7 + jnp.where(tm > 0, 1, 0))
     halo_copy = pltpu.make_async_remote_copy(
         src_ref=own,
         dst_ref=halo,
@@ -241,14 +241,23 @@
             device_id_type=MESH,
         )
 
-    def part_copy(a, b):
-        place = 4 * a + b
+    def x_copy(chunk, b):
         return pltpu.make_async_remote_copy(
-            src_ref=part_send.at[place],
-            dst_ref=part_recv.at[place],
-            send_sem=send_sem.at[place],
-            recv_sem=recv_sem.at[place],
-            device_id=at(a, b, core),
+            src_ref=x_send.at[b - 1, pl.ds(2 * chunk, 2)],
+            dst_ref=x_recv.at[b - 1, pl.ds(2 * chunk, 2)],
+            send_sem=x_sem.at[0, chunk, b - 1],
+            recv_sem=x_sem.at[1, chunk, b - 1],
+            device_id=at(0, b, core),
+            device_id_type=MESH,
+        )
+
+    def z_copy(a):
+        return pltpu.make_async_remote_copy(
+            src_ref=z_send.at[a - 1],
+            dst_ref=z_recv.at[a - 1],
+            send_sem=z_sem.at[0, a - 1],
+            recv_sem=z_sem.at[1, a - 1],
+            device_id=at(a, 0, core),
             device_id_type=MESH,
         )
 
@@ -269,30 +278,38 @@
         series[2 * c : 2 * c + 2, SLICE:WIDE] = halo[c].astype(jnp.float32)
     spread(NEAR, FULL, NEAR, WIDE)
 
-    copies = []
     for chunk, slot, side in stages:
         multiply(chunk, slot, side, NEAR, FULL)
         shift(chunk, slot, side, to_send if slot < 2 else to_own)
-        copy = half_copy(chunk)
         if slot < 2:
-            copy.start()
-            continue
-        copy.wait()
-        for g, (a, b) in enumerate(blocks(chunk)):
-            place = 8 * chunk + g
-            value = half_own[place] + half_recv[place].astype(jnp.float32)
-            if (a, b) == (0, 0):
-                part_own[...] = value
-            else:
-                part_send[4 * a + b] = value.astype(jnp.bfloat16)
-                part = part_copy(a, b)
-                part.start()
-                copies.append((4 * a + b, part))
-
-    total = part_own[...]
-    for place, part in copies:
-        part.wait()
-        total = total + part_recv[place].astype(jnp.float32)
+            half_copy(chunk).start()
+
+    def pair_sum(chunk, i, b):
+        place = 8 * chunk + 4 * i + (2, 1, 3, 0).index(b)
+        return half_own[place] + half_recv[place].astype(jnp.float32)
+
+    for chunk in range(2):
+        half_copy(chunk).wait()
+        for b in (2, 1, 3):
+            for i in range(2):
+                x_send[b - 1, 2 * chunk + i] = pair_sum(chunk, i, b).astype(jnp.bfloat16)
+            x_copy(chunk, b).start()
+        for i in range(2):
+            x_own[2 * chunk + i] = pair_sum(chunk, i, 0)
+    for chunk in range(2):
+        for b in (1, 3, 2):
+            x_copy(chunk, b).wait()
+        for i in range(2):
+            total = x_own[2 * chunk + i]
+            for b in range(3):
+                total = total + x_recv[b, 2 * chunk + i].astype(jnp.float32)
+            a = 3 - 2 * chunk - i
+            if a:
+                z_send[a - 1] = total.astype(jnp.bfloat16)
+                z_copy(a).start()
+    for a in (3, 2, 1):
+        z_copy(a).wait()
+        total = total + z_recv[a - 1].astype(jnp.float32)
     out[...] = total * scale
 
 
@@ -324,14 +341,16 @@
             pltpu.VMEM((16, 16, SLICE), jnp.bfloat16),
             pltpu.VMEM((16, 16, SLICE), jnp.bfloat16),
             pltpu.VMEM((16, 16, SLICE), jnp.float32),
-            pltpu.VMEM((16, 16, SLICE), jnp.bfloat16),
-            pltpu.VMEM((16, 16, SLICE), jnp.bfloat16),
-            pltpu.VMEM((16, SLICE), jnp.float32),
+            pltpu.VMEM((3, 4, 16, SLICE), jnp.bfloat16),
+            pltpu.VMEM((3, 4, 16, SLICE), jnp.bfloat16),
+            pltpu.VMEM((4, 16, SLICE), jnp.float32),
+            pltpu.VMEM((3, 16, SLICE), jnp.bfloat16),
+            pltpu.VMEM((3, 16, SLICE), jnp.bfloat16),
             pltpu.SemaphoreType.DMA((5,)),
             pltpu.SemaphoreType.DMA((2,)),
             pltpu.SemaphoreType.DMA((2, 2)),
-            pltpu.SemaphoreType.DMA((16,)),
-            pltpu.SemaphoreType.DMA((16,)),
+            pltpu.SemaphoreType.DMA((2, 2, 3)),
+            pltpu.SemaphoreType.DMA((2, 3)),
         ],
         compiler_params=pltpu.CompilerParams(
             collective_id=0, has_side_effects=True, vmem_limit_bytes=40 * 1024 * 1024

time: 25.2 us -> 25.3 us (level)
  no operation moved by 1% of the time
where the time goes in v3:
time: 25.3 us; the launch traced here: 25.2 us
  Pallas kernels  24.6 us (97%)
  local copies, waits for them, and re-layouts  0.62 us (2%)
    pallas_call x1, Pallas kernels, shards(): pl.pallas_call(functools.partial(kernel, scale), out_shape=jax.ShapeDtype...  24.6 us
    unnamed x1, local copies, waits for them, and re-layouts  0.62 us

profile of v3, /device:TPU:24, one launch (start us, length us, event | category | flops | bytes accessed | tf_op | source)
XLA Modules:
  0.0 25.2 jit_solution(10475320700398455280)
XLA Ops:
  0.0 24.6 %shard_map.55 = f32[16,512]{1,0:T(8,128)S(1)} custom-call(bf16[3600,128]{1,0:T(8,128)(2,1)} %bitcast.9, bf16[3,2,512]{2,1,0:T(2,128)(2,1)} %bitcast.10, s32[2,512]{1,0:T(2,128)} %bitcast.11, s32[2,3]{1,0:T(2,128)} %gap_start.1, s32[2,3]{1,0:T(2,128)} %gap_length.1), custom_call_target="tpu_custom_call" | custom-call | tf_op jit(solution)/shard_map/pallas_call | solution.py:322
  24.6 0.6 %copy.8 = f32[16,512]{1,0:T(8,128)} copy(f32[16,512]{1,0:T(8,128)S(1)} %shard_map.55) | data formatting | bytes 65536

commit v4 on v3

v4 whole, which is shorter than its diff:
```python
import functools
import math

import jax
import jax.numpy as jnp
from jax import lax
from jax.experimental import pallas as pl
from jax.experimental.pallas import tpu as pltpu
from jax.sharding import PartitionSpec as P

CHANNELS = 3
TEMPLATE_LEN = 150
TEMPLATES = 512
MAXMO = 256
NT = 4096
SLICE = 512
WIDE = 1024
FULL = SLICE + MAXMO
NEAR = 256
ROWS = 160
DEPTH = 512
MESH = pl.DeviceIdType.MESH


def paired(index, by):
    return (index, index + 1 - 2 * lax.rem(index, 2), lax.rem(index + 2, 4), 3 - index)[by]


def kernel(
    scale,
    templates,
    records,
    moveout,
    gap_start,
    gap_length,
    out,
    packed,
    unit32,
    unit_t,
    unit_in,
    own,
    moves,
    gaps,
    line_send,
    line_in,
    halo,
    series,
    rolled,
    inverse,
    hankel,
    corr,
    lag,
    x_send,
    x_recv,
    x_own,
    z_send,
    z_recv,
    local_sem,
    halo_sem,
    pair_sem,
    x_sem,
    z_sem,
):
    sta = lax.axis_index("sta")
    tm = lax.axis_index("tm")
    core = lax.rem(sta, 2)
    xx = lax.rem(sta // 2, 4)
    zz = sta // 8
    zs = [paired(zz, a) for a in range(4)]
    xs = [paired(xx, b) for b in range(4)]

    def at(a, b, c):
        return {"sta": zs[a] * 8 + xs[b] * 2 + c}

    sibling = at(0, 0, 1 - core)
    barrier = pltpu.get_barrier_semaphore()

    @pl.when(tm < 7)
    def _():
        for c in range(2):
            pl.semaphore_signal(
                barrier,
                inc=1,
                device_id={**at(0, 0, c), "tm": lax.rem(tm + 1, 8)},
                device_id_type=MESH,
            )

    for a, b in ((3, 0), (2, 0), (1, 0), (0, 2), (0, 1), (0, 3)):
        pl.semaphore_signal(barrier, inc=1, device_id=at(a, b, core), device_id_type=MESH)
    pl.semaphore_signal(barrier, inc=1, device_id=sibling, device_id_type=MESH)

    loads = [
        pltpu.make_async_copy(records, own, local_sem.at[0]),
        pltpu.make_async_copy(gap_start, gaps.at[0], local_sem.at[1]),
        pltpu.make_async_copy(gap_length, gaps.at[1], local_sem.at[2]),
        pltpu.make_async_copy(moveout, moves.at[0], local_sem.at[3]),
        pltpu.make_async_copy(templates, packed, local_sem.at[4]),
    ]
    for load in loads:
        load.start()

    @pl.when(tm == 7)
    def _():
        halo[...] = jnp.zeros_like(halo)

    for load in loads[:4]:
        load.wait()

    series[...] = jnp.zeros_like(series)
    for c in range(CHANNELS):
        series[0, 2 * c : 2 * c + 2, 0:SLICE] = own[c].astype(jnp.float32)
    line = lax.broadcasted_iota(jnp.int32, (8, SLICE), 0)
    position = lax.broadcasted_iota(jnp.int32, (8, SLICE), 1) + tm * SLICE
    first = jnp.zeros((8, SLICE), jnp.int32)
    length = jnp.zeros((8, SLICE), jnp.int32)
    for s in range(2):
        for c in range(CHANNELS):
            first = jnp.where(line == 2 * c + s, gaps[0, s, c], first)
            length = jnp.where(line == 2 * c + s, gaps[1, s, c], length)
    kept = ((position < first) | (position >= first + length)) & (position < NT)
    masked = jnp.where(kept, series[0, :, 0:SLICE], 0.0)
    series[0, :, 0:SLICE] = masked
    line_send[...] = jnp.concatenate(
        [masked[:, : SLICE // 2], masked[:, SLICE // 2 :]], axis=0
    ).astype(jnp.bfloat16)

    def unfold(value):
        wide = value.astype(jnp.float32)
        return jnp.concatenate([wide[:8], wide[8:]], axis=1)

    def halo_copy(other):
        to = 1 - core if other else core
        return pltpu.make_async_remote_copy(
            src_ref=line_send,
            dst_ref=halo.at[other],
            send_sem=halo_sem.at[0, other],
            recv_sem=halo_sem.at[1, other],
            device_id={**at(0, 0, to), "tm": lax.rem(tm + 7, 8)},
            device_id_type=MESH,
        )

    def to_sibling(source, target, index):
        return pltpu.make_async_remote_copy(
            src_ref=source,
            dst_ref=target,
            send_sem=pair_sem.at[0, index],
            recv_sem=pair_sem.at[1, index],
            device_id=sibling,
            device_id_type=MESH,
        )

    line_copy = to_sibling(line_send, line_in, 0)
    move_copy = to_sibling(moves.at[0], moves.at[1], 1)
    unit_copy = to_sibling(unit_t.at[:, :, 1 - core], unit_in, 2)

    pl.semaphore_wait(barrier, 7 + jnp.where(tm > 0, 2, 0))

    @pl.when(tm > 0)
    def _():
        halo_copy(0).start()
        halo_copy(1).start()

    line_copy.start()
    move_copy.start()

    def spread_moves(side):
        for s in range(2):
            for q in range(4):
                line = moves[side, s : s + 1, 128 * q : 128 * (q + 1)]
                lag[2 * side + s, 128 * q : 128 * (q + 1), :] = jnp.broadcast_to(line, (128, 128)).T

    spread_moves(0)
    loads[4].wait()

    unit32[3600:3680, :] = jnp.zeros((80, 128), jnp.float32)
    for c in range(CHANNELS):
        wide = packed[1200 * c : 1200 * (c + 1), :].astype(jnp.float32).reshape(150, 8, 128)
        norm = 1.0 / jnp.sqrt(jnp.sum(wide * wide, axis=0, keepdims=True) + 1e-06)
        unit32[1200 * c : 1200 * (c + 1), :] = (wide * norm).reshape(1200, 128)
    row = lax.broadcasted_iota(jnp.int32, (ROWS, 128), 0)
    for s in range(2):
        for q in range(4):
            parts = []
            for c in range(CHANNELS):
                taken = unit32[pl.ds(1200 * c + 2 * q + s, ROWS, stride=8), :]
                parts.append(jnp.where(row < TEMPLATE_LEN, taken, 0.0))
            parts.append(jnp.zeros((DEPTH - 3 * ROWS, 128), jnp.float32))
            block = jnp.concatenate(parts, axis=0).astype(jnp.bfloat16)
            unit_t[s, 4 * q : 4 * (q + 1)] = block.T.reshape(4, 2, 16, DEPTH)
    unit_copy.start()

    def spread(side, begin, end, base, stop):
        span = stop - base
        width = end - begin
        skip = begin - base
        masked = series[side, :, base:stop]

        def ahead(value, by):
            return pltpu.roll(value, span - by, 1) if by else value

        eights = [ahead(masked, r) for r in range(8)]
        for r in range(8):
            for b in range(span // 128):
                rolled[side, b, 8 * r : 8 * (r + 1), :] = eights[r][:, 128 * b : 128 * (b + 1)]

        def tree(values):
            while len(values) > 1:
                values = [sum(values[i + 1 : i + 2], values[i]) for i in range(0, len(values), 2)]
            return values[0]

        squares = [value * value for value in eights]
        six = tree(squares[:6])
        eight_sum = six + (squares[6] + squares[7])
        most = tree([ahead(eight_sum, 8 * i) for i in range(8)])
        rest = tree([ahead(eight_sum, 128), ahead(eight_sum, 136), ahead(six, 144)])
        energy = (most + ahead(most, 64)) + rest
        inverse[side, :, begin:end] = (1.0 / jnp.sqrt(jnp.maximum(energy, 1.0)))[:, skip : skip + width]
        for s in range(2):
            hankel[2 * side + s, 3 * ROWS : DEPTH, begin:end] = jnp.zeros(
                (DEPTH - 3 * ROWS, width), jnp.bfloat16
            )
            for c in range(CHANNELS):
                eight = jnp.concatenate(
                    [rolled[side, b, pl.ds(2 * c + s, 8, stride=8), :] for b in range(span // 128)],
                    axis=1,
                )
                weight = inverse[side, 2 * c + s : 2 * c + s + 1, begin:end]
                for g in range(ROWS // 16):
                    pair = [
                        ahead(eight, 16 * g + 8 * h)[:, skip : skip + width] * weight
                        for h in range(2)
                    ]
                    hankel[
                        2 * side + s, ROWS * c + 16 * g : ROWS * c + 16 * (g + 1), begin:end
                    ] = (
                        jnp.concatenate(pair, axis=0).astype(jnp.bfloat16)
                    )

    def blocks(chunk):
        return [(a, b) for a in ((3, 2), (1, 0))[chunk] for b in (2, 1, 3, 0)]

    def multiply(side, chunk, begin, end):
        for s in range(2):
            rows = []
            for a, b in blocks(chunk):
                block = 4 * zs[a] + xs[b]
                rows.append(unit_in[s, block] if side else unit_t[s, block, core])
            corr[2 * side + s, 128 * chunk : 128 * (chunk + 1), begin:end] = jnp.dot(
                jnp.concatenate(rows, axis=0),
                hankel[2 * side + s, :, begin:end],
                preferred_element_type=jnp.float32,
            )

    lane = lax.broadcasted_iota(jnp.int32, (16, 128), 1)

    def shift(chunk):
        for g, (a, b) in enumerate(blocks(chunk)):
            base = 128 * chunk + 16 * g
            start = pl.multiple_of(128 * zs[a] + 32 * xs[b] + 16 * core, 16)
            total = [None] * 4
            for s in range(4):
                move = lag[s, pl.ds(start, 16), :]
                near = move <= lane
                middle = move <= lane + 128
                index = (lane + move) & 127
                pieces = [corr[s, base : base + 16, 128 * j : 128 * (j + 1)] for j in range(6)]
                for j in range(4):
                    mixed = jnp.where(
                        near, pieces[j], jnp.where(middle, pieces[j + 1], pieces[j + 2])
                    )
                    moved = jnp.take_along_axis(mixed, index, axis=1, mode="promise_in_bounds")
                    total[j] = moved if s == 0 else total[j] + moved
            value = jnp.concatenate(total, axis=1)
            if b:
                x_send[b - 1, 3 - a] = value.astype(jnp.bfloat16)
            else:
                x_own[3 - a] = value

    def x_copy(chunk, b):
        return pltpu.make_async_remote_copy(
            src_ref=x_send.at[b - 1, pl.ds(2 * chunk, 2)],
            dst_ref=x_recv.at[b - 1, pl.ds(2 * chunk, 2)],
            send_sem=x_sem.at[0, chunk, b - 1],
            recv_sem=x_sem.at[1, chunk, b - 1],
            device_id=at(0, b, core),
            device_id_type=MESH,
        )

    def z_copy(a):
        return pltpu.make_async_remote_copy(
            src_ref=z_send.at[a - 1],
            dst_ref=z_recv.at[a - 1],
            send_sem=z_sem.at[0, a - 1],
            recv_sem=z_sem.at[1, a - 1],
            device_id=at(a, 0, core),
            device_id_type=MESH,
        )

    spread(0, 0, NEAR, 0, SLICE)
    for chunk in range(2):
        multiply(0, chunk, 0, NEAR)
    line_copy.wait()
    move_copy.wait()
    series[1, :, 0:SLICE] = unfold(line_in[...])
    spread_moves(1)
    spread(1, 0, NEAR, 0, SLICE)
    unit_copy.wait()
    for chunk in range(2):
        multiply(1, chunk, 0, NEAR)

    @pl.when(tm > 0)
    def _():
        for other in range(2):
            halo_copy(other).wait_send()

    @pl.when(tm < 7)
    def _():
        for other in (1, 0):
            halo_copy(other).wait_recv()

    for side in range(2):
        series[side, :, SLICE:WIDE] = unfold(halo[side])
        spread(side, NEAR, FULL, NEAR, WIDE)
    for chunk in range(2):
        for side in range(2):
            multiply(side, chunk, NEAR, FULL)
        shift(chunk)
        for b in (2, 1, 3):
            x_copy(chunk, b).start()
    for chunk in range(2):
        for b in (1, 3, 2):
            x_copy(chunk, b).wait()
        for i in range(2):
            total = x_own[2 * chunk + i]
            for b in range(3):
                total = total + x_recv[b, 2 * chunk + i].astype(jnp.float32)
            a = 3 - 2 * chunk - i
            if a:
                z_send[a - 1] = total.astype(jnp.bfloat16)
                z_copy(a).start()
    for a in (3, 2, 1):
        z_copy(a).wait()
        total = total + z_recv[a - 1].astype(jnp.float32)
    out[...] = total * scale


def shards(records, templates, moveout, gap_start, gap_length):
    stations = records.shape[0] * lax.axis_size("sta")
    scale = math.sqrt(TEMPLATE_LEN / (3.0 * stations))
    lines = jnp.transpose(templates, (2, 3, 1, 0)).reshape(450, 2, 4, 128)
    lines = jnp.transpose(lines, (0, 2, 1, 3)).reshape(3600, 128)
    whole = pl.BlockSpec(memory_space=pltpu.HBM)
    return pl.pallas_call(
        functools.partial(kernel, scale),
        out_shape=jax.ShapeDtypeStruct((16, SLICE), jnp.float32),
        in_specs=[whole] * 5,
        out_specs=pl.BlockSpec(memory_space=pltpu.VMEM),
        scratch_shapes=[
            pltpu.VMEM((3600, 128), jnp.bfloat16),
            pltpu.VMEM((3680, 128), jnp.float32),
            pltpu.VMEM((2, 16, 2, 16, DEPTH), jnp.bfloat16),
            pltpu.VMEM((2, 16, 16, DEPTH), jnp.bfloat16),
            pltpu.VMEM((3, 2, SLICE), jnp.bfloat16),
            pltpu.VMEM((2, 2, TEMPLATES), jnp.int32),
            pltpu.SMEM((2, 2, 3), jnp.int32),
            pltpu.VMEM((16, SLICE // 2), jnp.bfloat16),
            pltpu.VMEM((16, SLICE // 2), jnp.bfloat16),
            pltpu.VMEM((2, 16, SLICE // 2), jnp.bfloat16),
            pltpu.VMEM((2, 8, WIDE), jnp.float32),
            pltpu.VMEM((2, 8, 64, 128), jnp.float32),
            pltpu.VMEM((2, 8, FULL), jnp.float32),
            pltpu.VMEM((4, DEPTH, FULL), jnp.bfloat16),
            pltpu.VMEM((4, TEMPLATES // 2, FULL), jnp.float32),
            pltpu.VMEM((4, TEMPLATES, 128), jnp.int32),
            pltpu.VMEM((3, 4, 16, SLICE), jnp.bfloat16),
            pltpu.VMEM((3, 4, 16, SLICE), jnp.bfloat16),
            pltpu.VMEM((4, 16, SLICE), jnp.float32),
            pltpu.VMEM((3, 16, SLICE), jnp.bfloat16),
            pltpu.VMEM((3, 16, SLICE), jnp.bfloat16),
            pltpu.SemaphoreType.DMA((5,)),
            pltpu.SemaphoreType.DMA((2, 2)),
            pltpu.SemaphoreType.DMA((2, 3)),
            pltpu.SemaphoreType.DMA((2, 2, 3)),
            pltpu.SemaphoreType.DMA((2, 3)),
        ],
        compiler_params=pltpu.CompilerParams(
            collective_id=0, has_side_effects=True, vmem_limit_bytes=40 * 1024 * 1024
        ),
    )(
        *[
            pltpu.with_memory_space_constraint(value, pltpu.HBM)
            for value in (
                lines,
                jnp.transpose(records, (1, 0, 2)),
                jnp.transpose(moveout, (1, 0)),
                gap_start,
                gap_length,
            )
        ]
    )


def solution(mesh):
    placed = (
        P("sta", None, "tm"),
        P(None, "sta", None, None),
        P(None, "sta"),
        P("sta", None),
        P("sta", None),
    )
    return jax.shard_map(
        shards, mesh=mesh, in_specs=placed, out_specs=P("sta", "tm"), check_vma=False
    )
```

time: 25.3 us -> 25.1 us (level)
  no operation moved by 1% of the time
where the time goes in v4:
time: 25.1 us; the launch traced here: 25 us
  Pallas kernels  24.4 us (97%)
  local copies, waits for them, and re-layouts  0.62 us (2%)
    pallas_call x1, Pallas kernels, shards(): pl.pallas_call(functools.partial(kernel, scale), out_shape=jax.ShapeDtype...  24.4 us
    unnamed x1, local copies, waits for them, and re-layouts  0.62 us

profile of v4, /device:TPU:24, one launch (start us, length us, event | category | flops | bytes accessed | tf_op | source)
XLA Modules:
  0.0 25.0 jit_solution(57859805964028378)
XLA Ops:
  0.0 24.4 %shard_map.55 = f32[16,512]{1,0:T(8,128)S(1)} custom-call(bf16[3600,128]{1,0:T(8,128)(2,1)} %bitcast.9, bf16[3,2,512]{2,1,0:T(2,128)(2,1)} %bitcast.10, s32[2,512]{1,0:T(2,128)} %bitcast.11, s32[2,3]{1,0:T(2,128)} %gap_start.1, s32[2,3]{1,0:T(2,128)} %gap_length.1), custom_call_target="tpu_custom_call" | custom-call | tf_op jit(solution)/shard_map/pallas_call | solution.py:353
  24.4 0.6 %copy.8 = f32[16,512]{1,0:T(8,128)} copy(f32[16,512]{1,0:T(8,128)S(1)} %shard_map.55) | data formatting | bytes 65536

commit v5 on v4

--- a/solution.py
+++ b/solution.py
@@ -41,8 +41,7 @@
     own,
     moves,
     gaps,
-    line_send,
-    line_in,
+    lines,
     halo,
     series,
     rolled,
@@ -75,15 +74,13 @@
     sibling = at(0, 0, 1 - core)
     barrier = pltpu.get_barrier_semaphore()
 
-    @pl.when(tm < 7)
-    def _():
-        for c in range(2):
-            pl.semaphore_signal(
-                barrier,
-                inc=1,
-                device_id={**at(0, 0, c), "tm": lax.rem(tm + 1, 8)},
-                device_id_type=MESH,
-            )
+    through = core == 1
+
+    @pl.when(through & (tm < 7))
+    def _():
+        pl.semaphore_signal(
+            barrier, inc=1, device_id={"tm": lax.rem(tm + 1, 8)}, device_id_type=MESH
+        )
 
     for a, b in ((3, 0), (2, 0), (1, 0), (0, 2), (0, 1), (0, 3)):
         pl.semaphore_signal(barrier, inc=1, device_id=at(a, b, core), device_id_type=MESH)
@@ -108,7 +105,7 @@
 
     series[...] = jnp.zeros_like(series)
     for c in range(CHANNELS):
-        series[0, 2 * c : 2 * c + 2, 0:SLICE] = own[c].astype(jnp.float32)
+        series[2 * c : 2 * c + 2, 0:SLICE] = own[c].astype(jnp.float32)
     line = lax.broadcasted_iota(jnp.int32, (8, SLICE), 0)
     position = lax.broadcasted_iota(jnp.int32, (8, SLICE), 1) + tm * SLICE
     first = jnp.zeros((8, SLICE), jnp.int32)
@@ -118,9 +115,9 @@
             first = jnp.where(line == 2 * c + s, gaps[0, s, c], first)
             length = jnp.where(line == 2 * c + s, gaps[1, s, c], length)
     kept = ((position < first) | (position >= first + length)) & (position < NT)
-    masked = jnp.where(kept, series[0, :, 0:SLICE], 0.0)
-    series[0, :, 0:SLICE] = masked
-    line_send[...] = jnp.concatenate(
+    masked = jnp.where(kept, series[0:8, 0:SLICE], 0.0)
+    series[0:8, 0:SLICE] = masked
+    lines[core] = jnp.concatenate(
         [masked[:, : SLICE // 2], masked[:, SLICE // 2 :]], axis=0
     ).astype(jnp.bfloat16)
 
@@ -128,16 +125,14 @@
         wide = value.astype(jnp.float32)
         return jnp.concatenate([wide[:8], wide[8:]], axis=1)
 
-    def halo_copy(other):
-        to = 1 - core if other else core
-        return pltpu.make_async_remote_copy(
-            src_ref=line_send,
-            dst_ref=halo.at[other],
-            send_sem=halo_sem.at[0, other],
-            recv_sem=halo_sem.at[1, other],
-            device_id={**at(0, 0, to), "tm": lax.rem(tm + 7, 8)},
-            device_id_type=MESH,
-        )
+    halo_copy = pltpu.make_async_remote_copy(
+        src_ref=lines,
+        dst_ref=halo,
+        send_sem=halo_sem.at[0],
+        recv_sem=halo_sem.at[1],
+        device_id={"tm": lax.rem(tm + 7, 8)},
+        device_id_type=MESH,
+    )
 
     def to_sibling(source, target, index):
         return pltpu.make_async_remote_copy(
@@ -149,18 +144,20 @@
             device_id_type=MESH,
         )
 
-    line_copy = to_sibling(line_send, line_in, 0)
+    line_copy = to_sibling(lines.at[core], lines.at[core], 0)
     move_copy = to_sibling(moves.at[0], moves.at[1], 1)
     unit_copy = to_sibling(unit_t.at[:, :, 1 - core], unit_in, 2)
 
-    pl.semaphore_wait(barrier, 7 + jnp.where(tm > 0, 2, 0))
-
-    @pl.when(tm > 0)
-    def _():
-        halo_copy(0).start()
-        halo_copy(1).start()
-
+    hand_on = to_sibling(halo, halo, 3)
+    sends = through & (tm > 0)
+    pl.semaphore_wait(barrier, 7 + jnp.where(sends, 1, 0))
     line_copy.start()
+
+    @pl.when(sends)
+    def _():
+        line_copy.wait_recv()
+        halo_copy.start()
+
     move_copy.start()
 
     def spread_moves(side):
@@ -189,52 +186,46 @@
             unit_t[s, 4 * q : 4 * (q + 1)] = block.T.reshape(4, 2, 16, DEPTH)
     unit_copy.start()
 
-    def spread(side, begin, end, base, stop):
+    def spread(begin, end, base, stop):
         span = stop - base
         width = end - begin
         skip = begin - base
-        masked = series[side, :, base:stop]
+        masked = series[:, base:stop].astype(jnp.bfloat16)
 
         def ahead(value, by):
             return pltpu.roll(value, span - by, 1) if by else value
 
-        eights = [ahead(masked, r) for r in range(8)]
-        for r in range(8):
+        rows = [ahead(masked, r).astype(jnp.float32) for r in range(16)]
+        for r in range(16):
             for b in range(span // 128):
-                rolled[side, b, 8 * r : 8 * (r + 1), :] = eights[r][:, 128 * b : 128 * (b + 1)]
-
-        def tree(values):
-            while len(values) > 1:
-                values = [sum(values[i + 1 : i + 2], values[i]) for i in range(0, len(values), 2)]
-            return values[0]
-
-        squares = [value * value for value in eights]
-        six = tree(squares[:6])
-        eight_sum = six + (squares[6] + squares[7])
-        most = tree([ahead(eight_sum, 8 * i) for i in range(8)])
-        rest = tree([ahead(eight_sum, 128), ahead(eight_sum, 136), ahead(six, 144)])
-        energy = (most + ahead(most, 64)) + rest
-        inverse[side, :, begin:end] = (1.0 / jnp.sqrt(jnp.maximum(energy, 1.0)))[:, skip : skip + width]
-        for s in range(2):
-            hankel[2 * side + s, 3 * ROWS : DEPTH, begin:end] = jnp.zeros(
+                rolled[b, 16 * r : 16 * (r + 1), :] = rows[r][:, 128 * b : 128 * (b + 1)]
+        squares = [value * value for value in rows[:8]]
+        six = ((squares[0] + squares[1]) + (squares[2] + squares[3])) + (squares[4] + squares[5])
+        over8 = six + (squares[6] + squares[7])
+        over16 = over8 + ahead(over8, 8)
+        over32 = over16 + (ahead(over8, 16) + ahead(over8, 24))
+        over128 = (over32 + ahead(over32, 32)) + (ahead(over32, 64) + ahead(over32, 96))
+        energy = over128 + (ahead(over16, 128) + ahead(six, 144))
+        inverse[:, begin:end] = (1.0 / jnp.sqrt(jnp.maximum(energy, 1.0)))[:, skip : skip + width]
+        for s in range(4):
+            hankel[s, 3 * ROWS : DEPTH, begin:end] = jnp.zeros(
                 (DEPTH - 3 * ROWS, width), jnp.bfloat16
             )
             for c in range(CHANNELS):
-                eight = jnp.concatenate(
-                    [rolled[side, b, pl.ds(2 * c + s, 8, stride=8), :] for b in range(span // 128)],
+                line = 8 * (s // 2) + 2 * c + s % 2
+                sixteen = jnp.concatenate(
+                    [rolled[b, pl.ds(line, 16, stride=16), :] for b in range(span // 128)],
                     axis=1,
-                )
-                weight = inverse[side, 2 * c + s : 2 * c + s + 1, begin:end]
-                for g in range(ROWS // 16):
-                    pair = [
-                        ahead(eight, 16 * g + 8 * h)[:, skip : skip + width] * weight
-                        for h in range(2)
-                    ]
-                    hankel[
-                        2 * side + s, ROWS * c + 16 * g : ROWS * c + 16 * (g + 1), begin:end
-                    ] = (
-                        jnp.concatenate(pair, axis=0).astype(jnp.bfloat16)
-                    )
+                ).astype(jnp.bfloat16)
+                weight = inverse[line : line + 1, begin:end]
+                for b in range(8):
+                    moved = ahead(sixteen, 16 * b)
+                    for h in range(2 if b < 2 else 1):
+                        top = ROWS * c + 16 * b + 128 * h
+                        taken = moved[:, skip + 128 * h : skip + 128 * h + width]
+                        hankel[s, top : top + 16, begin:end] = (
+                            taken.astype(jnp.float32) * weight
+                        ).astype(jnp.bfloat16)
 
     def blocks(chunk):
         return [(a, b) for a in ((3, 2), (1, 0))[chunk] for b in (2, 1, 3, 0)]
@@ -296,31 +287,37 @@
             device_id_type=MESH,
         )
 
-    spread(0, 0, NEAR, 0, SLICE)
+    @pl.when(jnp.logical_not(sends))
+    def _():
+        line_copy.wait_recv()
+
+    line_copy.wait_send()
+    move_copy.wait()
+    series[8:16, 0:SLICE] = unfold(lines[1 - core])
+    spread_moves(1)
+    spread(0, NEAR, 0, SLICE)
     for chunk in range(2):
         multiply(0, chunk, 0, NEAR)
-    line_copy.wait()
-    move_copy.wait()
-    series[1, :, 0:SLICE] = unfold(line_in[...])
-    spread_moves(1)
-    spread(1, 0, NEAR, 0, SLICE)
     unit_copy.wait()
     for chunk in range(2):
         multiply(1, chunk, 0, NEAR)
 
-    @pl.when(tm > 0)
-    def _():
-        for other in range(2):
-            halo_copy(other).wait_send()
-
-    @pl.when(tm < 7)
-    def _():
-        for other in (1, 0):
-            halo_copy(other).wait_recv()
-
-    for side in range(2):
-        series[side, :, SLICE:WIDE] = unfold(halo[side])
-        spread(side, NEAR, FULL, NEAR, WIDE)
+    @pl.when(sends)
+    def _():
+        halo_copy.wait_send()
+
+    @pl.when(through & (tm < 7))
+    def _():
+        halo_copy.wait_recv()
+        hand_on.start()
+
+    @pl.when((core == 0) & (tm < 7))
+    def _():
+        hand_on.wait_recv()
+
+    series[0:8, SLICE:WIDE] = unfold(halo[core])
+    series[8:16, SLICE:WIDE] = unfold(halo[1 - core])
+    spread(NEAR, FULL, NEAR, WIDE)
     for chunk in range(2):
         for side in range(2):
             multiply(side, chunk, NEAR, FULL)
@@ -343,6 +340,10 @@
         total = total + z_recv[a - 1].astype(jnp.float32)
     out[...] = total * scale
 
+    @pl.when(through & (tm < 7))
+    def _():
+        hand_on.wait_send()
+
 
 def shards(records, templates, moveout, gap_start, gap_length):
     stations = records.shape[0] * lax.axis_size("sta")
@@ -363,12 +364,11 @@
             pltpu.VMEM((3, 2, SLICE), jnp.bfloat16),
             pltpu.VMEM((2, 2, TEMPLATES), jnp.int32),
             pltpu.SMEM((2, 2, 3), jnp.int32),
-            pltpu.VMEM((16, SLICE // 2), jnp.bfloat16),
-            pltpu.VMEM((16, SLICE // 2), jnp.bfloat16),
             pltpu.VMEM((2, 16, SLICE // 2), jnp.bfloat16),
-            pltpu.VMEM((2, 8, WIDE), jnp.float32),
-            pltpu.VMEM((2, 8, 64, 128), jnp.float32),
-            pltpu.VMEM((2, 8, FULL), jnp.float32),
+            pltpu.VMEM((2, 16, SLICE // 2), jnp.bfloat16),
+            pltpu.VMEM((16, WIDE), jnp.float32),
+            pltpu.VMEM((8, 256, 128), jnp.float32),
+            pltpu.VMEM((16, FULL), jnp.float32),
             pltpu.VMEM((4, DEPTH, FULL), jnp.bfloat16),
             pltpu.VMEM((4, TEMPLATES // 2, FULL), jnp.float32),
             pltpu.VMEM((4, TEMPLATES, 128), jnp.int32),
@@ -378,8 +378,8 @@
             pltpu.VMEM((3, 16, SLICE), jnp.bfloat16),
             pltpu.VMEM((3, 16, SLICE), jnp.bfloat16),
             pltpu.SemaphoreType.DMA((5,)),
-            pltpu.SemaphoreType.DMA((2, 2)),
-            pltpu.SemaphoreType.DMA((2, 3)),
+            pltpu.SemaphoreType.DMA((2,)),
+            pltpu.SemaphoreType.DMA((2, 4)),
             pltpu.SemaphoreType.DMA((2, 2, 3)),
             pltpu.SemaphoreType.DMA((2, 3)),
         ],

time: 25.1 us -> 23.4 us (0.932)
  Pallas kernels: 24.4 us -> 22.7 us
    pallas_call x1, Pallas kernels: 24.4 us -> 22.7 us  [shards(): pl.pallas_call(functools.partial(kernel, scale), out_shape=jax.ShapeDtype...]
where the time goes in v5:
time: 23.4 us; the launch traced here: 23.3 us
  Pallas kernels  22.7 us (97%)
  local copies, waits for them, and re-layouts  0.62 us (3%)
    pallas_call x1, Pallas kernels, shards(): pl.pallas_call(functools.partial(kernel, scale), out_shape=jax.ShapeDtype...  22.7 us
    unnamed x1, local copies, waits for them, and re-layouts  0.62 us

profile of v5, /device:TPU:24, one launch (start us, length us, event | category | flops | bytes accessed | tf_op | source)
XLA Modules:
  0.0 23.3 jit_solution(1457788541128047145)
XLA Ops:
  0.0 22.7 %shard_map.55 = f32[16,512]{1,0:T(8,128)S(1)} custom-call(bf16[3600,128]{1,0:T(8,128)(2,1)} %bitcast.9, bf16[3,2,512]{2,1,0:T(2,128)(2,1)} %bitcast.10, s32[2,512]{1,0:T(2,128)} %bitcast.11, s32[2,3]{1,0:T(2,128)} %gap_start.1, s32[2,3]{1,0:T(2,128)} %gap_length.1), custom_call_target="tpu_custom_call" | custom-call | tf_op jit(solution)/shard_map/pallas_call | solution.py:354
  22.7 0.6 %copy.8 = f32[16,512]{1,0:T(8,128)} copy(f32[16,512]{1,0:T(8,128)S(1)} %shard_map.55) | data formatting | bytes 65536
